TPU v7x, 512 devices: a whole 4x8x8 slice. The times are simulated.
512 devices in a mesh: expert: 8 (over x, z_hi), dp: 64 (over y, z_lo, core).
Axes of the slice: x: 4, y: 8, z: 8 (z_hi: 2, z_lo: 4; z = z_hi * 4 + z_lo), core: 2. Of those that a mesh axis runs over, the one named last changes fastest.
Arguments:
- output_gradient: bfloat16 [2048, 6144], P(('expert', 'dp')), may hold values from -6 to 6
- gates: float32 [2048, 2], P(('expert', 'dp')), may hold values from 0.2 to 1
- expert_index: int32 [2048, 2], P(('expert', 'dp')), may hold values from 0 to 7, all different within a row; in each aligned block of 4 rows (0 to 3, 4 to 7, ...) at most 2 rows name the same one
- hidden_state: bfloat16 [8, 1024, 16384], P('expert', None, 'dp'), may hold values from -6 to 6
- down_matrix: bfloat16 [8, 16384, 6144], P('expert', 'dp'), may hold values from -0.078125 to 0.078125
- left_adapter: bfloat16 [8, 16384, 16], P('expert', 'dp'), may hold values from -0.046875 to 0.046875
- right_adapter: bfloat16 [8, 16, 6144], P('expert'), may hold values from -0.078125 to 0.078125
Outputs:
- hidden_gradient: bfloat16 [8, 1024, 16384], P('expert', None, 'dp')
- left_gradient: float32 [8, 16384, 16], P('expert', 'dp')
- right_gradient: float32 [8, 16, 6144], P('expert')
Inputs may be any that keep to these rules, and one draw needn't show every extreme that they name: `expert_index`: each token names 2 different experts; the tokens of one device name one expert at most 2 times.
All inputs are finite; a program needn't handle non-finite values.
Results may differ from a plain program's by a relative error of at most 0.0049.
Values may be sent and summed in bfloat16 or wider, within the bound.
A program may use at most 128 MiB of HBM per device.

v0:
```python
import jax
import jax.numpy as jnp
from jax import lax
from jax.sharding import PartitionSpec as P

adapter_scale = 2.0


def shards(
    output_gradient, gates, expert_index, hidden_state, down_matrix, left_adapter, right_adapter
):
    expert_count = lax.axis_size("expert")
    group_count = lax.axis_size("dp")
    width = output_gradient.shape[1]
    capacity = hidden_state.shape[1] // (expert_count * group_count)
    scaled = (
        (gates[:, :, None] * output_gradient[:, None, :].astype(jnp.float32))
        .astype(jnp.bfloat16)
        .reshape(-1, width)
    )
    chosen = expert_index.reshape(-1)
    onehot = (chosen[:, None] == jnp.arange(expert_count, dtype=jnp.int32)[None, :]).astype(
        jnp.int32
    )
    position = jnp.sum((jnp.cumsum(onehot, axis=0) - onehot) * onehot, axis=1)
    send_buffer = jnp.zeros((expert_count * capacity, width), jnp.bfloat16)
    send_buffer = (
        send_buffer.at[chosen * capacity + position]
        .set(scaled)
        .reshape(expert_count, capacity, width)
    )
    arrived = lax.all_to_all(send_buffer, "expert", split_axis=0, concat_axis=0, tiled=True)
    gathered = lax.all_gather(arrived.reshape(-1, width), "dp", axis=0, tiled=True)
    weight_slice = down_matrix[0]
    left_factor = left_adapter[0]
    right_factor = right_adapter[0]
    gated_input = hidden_state[0]
    reduced_rows = lax.dot_general(
        gathered, right_factor, (((1,), (1,)), ((), ())), preferred_element_type=jnp.float32
    ).astype(jnp.bfloat16)
    frozen_path = lax.dot_general(
        gathered, weight_slice, (((1,), (1,)), ((), ())), preferred_element_type=jnp.float32
    )
    adapter_delta = lax.dot_general(
        reduced_rows, left_factor, (((1,), (1,)), ((), ())), preferred_element_type=jnp.float32
    )
    hidden_gradient = (frozen_path + adapter_scale * adapter_delta).astype(jnp.bfloat16)
    left_gradient = adapter_scale * lax.dot_general(
        gated_input, reduced_rows, (((0,), (0,)), ((), ())), preferred_element_type=jnp.float32
    )
    factor_part = jnp.dot(gated_input, left_factor, preferred_element_type=jnp.float32)
    own_count = gathered.shape[0] // group_count
    own_factor = lax.psum_scatter(factor_part, "dp", scatter_dimension=0, tiled=True).astype(
        jnp.bfloat16
    )
    own_rows = lax.dynamic_slice_in_dim(gathered, lax.axis_index("dp") * own_count, own_count, 0)
    partial_right = adapter_scale * lax.dot_general(
        own_factor, own_rows, (((0,), (0,)), ((), ())), preferred_element_type=jnp.float32
    )
    right_gradient = lax.psum(partial_right, "dp")
    return (hidden_gradient[None], left_gradient[None], right_gradient[None])


def solution(mesh):
    in_specs = (
        P(("expert", "dp"), None),
        P(("expert", "dp"), None),
        P(("expert", "dp"), None),
        P("expert", None, "dp"),
        P("expert", "dp", None),
        P("expert", "dp", None),
        P("expert", None, None),
    )
    out_specs = (P("expert", None, "dp"), P("expert", "dp", None), P("expert", None, None))
    return jax.shard_map(shards, mesh=mesh, in_specs=in_specs, out_specs=out_specs, check_vma=False)
```

profile of v0, /device:TPU:1, one launch (start us, length us, event | category | flops | bytes accessed | tf_op | source)
XLA Modules:
  0.0 969.0 jit_solution(9862416301830627037)
XLA Ops:
  7.2 0.0 copy-start
  7.2 0.9 copy.17
  8.1 0.7 broadcast_multiply_fusion
  8.8 0.1 eq.15
  8.9 0.1 fusion.18
  9.0 0.2 select_reduce_fusion
  9.2 0.1 copy.16
  9.3 0.1 mul.59
  9.4 0.9 mul.63
  10.2 0.1 mul.64
  10.4 0.8 copy.18
  11.1 0.1 mul.61
  11.2 0.9 scatter_custom_fusion
  12.1 0.8 reshape.49
  12.9 13.3 %all-to-all-start = ((bf16[8,2,6144]{2,1,0:T(2,128)(2,1)}), bf16[8,2,6144]{2,1,0:T(2,128)(2,1)S(1)}, u32[]{:S(2)}, u32[]{:S(2)}) async-start(bf16[8,2,6144]{2,1,0:T(2,128)(2,1)} %reshape.49), calls=%async_computation | async-start | bytes 393216 | tf_op jit(solution)/shard_map/all_to_all | solution.py:32
  26.2 0.0 reduce-scatter.2.cloned.1.call-start
  26.3 2.1 fusion.7
  28.4 0.0 reduce-scatter.2.cloned.1.call-update
  28.4 0.0 copy-start.3
  28.4 0.0 all-gather.2.cloned.1.call-start
  28.5 7.5 all-to-all-done
  36.0 0.8 reshape.50
  36.8 0.0 all-gather.2.cloned.1.call-update
  36.8 0.0 all-reduce.2.cloned.1.call-start
  36.8 271.4 %reduce-scatter.2.cloned.1.call-done = f32[16,16]{1,0:T(8,128)} async-done(((f32[1024,16]{1,0:T(8,128)}), f32[16,16]{1,0:T(8,128)}) %reduce-scatter.2.cloned.1.call-update) | async-done | bytes 1040 | tf_op jit(solution)/shard_map/reduce_scatter | solution.py:53
  308.2 136.4 %all-gather.2.cloned.1.call-done = bf16[1024,6144]{1,0:T(8,128)(2,1)} async-done(((bf16[16,6144]{1,0:T(8,128)(2,1)}), bf16[1024,6144]{1,0:T(8,128)(2,1)}) %all-gather.2.cloned.1.call-update) | async-done | bytes 12582928 | tf_op jit(solution)/shard_map/all_gather | solution.py:33
  444.6 1.9 fusion
  446.5 0.0 all-reduce.2.cloned.1.call-update
  446.5 0.0 copy-done
  446.5 0.0 copy-start.1
  446.5 7.8 fusion.1
  454.3 0.0 copy-done.3
  454.3 0.4 copy-done.1
  454.7 0.0 copy-start.2
  454.7 0.0 copy-start.4
  454.7 3.3 convolution_convert_fusion
  458.0 0.0 copy-done.2
  458.0 0.8 fusion.6
  458.9 0.0 copy-done.4
  458.9 1.1 fusion.5
  460.0 500.8 %all-reduce.2.cloned.1.call-done = f32[1,16,6144]{2,1,0:T(8,128)} async-done(((f32[1,16,6144]{2,1,0:T(8,128)}), f32[1,16,6144]{2,1,0:T(8,128)}) %all-reduce.2.cloned.1.call-update) | async-done | bytes 393232 | tf_op jit(solution)/shard_map/psum | solution.py:60
  960.7 1.8 copy.20
  (2 shorter events, 0.0 us)
Async XLA Ops:
  7.2 439.3 %copy-start = (bf16[1,256,6144]{2,1,0:T(8,128)(2,1)S(1)}, bf16[1,256,6144]{2,1,0:T(8,128)(2,1)}, u32[]{:S(2)}) copy-start(bf16[1,256,6144]{2,1,0:T(8,128)(2,1)} %param.11) | copy-start | bytes 9437188
  12.9 23.1 %all-to-all-start = ((bf16[8,2,6144]{2,1,0:T(2,128)(2,1)}), bf16[8,2,6144]{2,1,0:T(2,128)(2,1)S(1)}, u32[]{:S(2)}, u32[]{:S(2)}) async-start(bf16[8,2,6144]{2,1,0:T(2,128)(2,1)} %reshape.49), calls=%async_computation | async-start | bytes 393216 | tf_op jit(solution)/shard_map/all_to_all | solution.py:32
  26.2 282.0 %reduce-scatter.2.cloned.1.call-start = ((), (), s32[]{:S(2)}) async-start(), calls=%async_computation.3 | async-start | bytes 532480 | tf_op jit(solution)/shard_map/reduce_scatter | solution.py:53
  28.4 425.9 %copy-start.3 = (bf16[1,16,6144]{2,1,0:T(8,128)(2,1)S(1)}, bf16[1,16,6144]{2,1,0:T(8,128)(2,1)}, u32[]{:S(2)}) copy-start(bf16[1,16,6144]{2,1,0:T(8,128)(2,1)} %param.13) | copy-start | bytes 589828
  28.4 416.2 %all-gather.2.cloned.1.call-start = ((), (), s32[]{:S(2)}) async-start(), calls=%async_computation.2 | async-start | bytes 12779520 | tf_op jit(solution)/shard_map/all_gather | solution.py:33
  36.8 924.0 %all-reduce.2.cloned.1.call-start = ((), (), s32[]{:S(2)}) async-start(), calls=%async_computation.4 | async-start | bytes 786432 | tf_op jit(solution)/shard_map/psum | solution.py:60
  446.5 8.2 copy-start.1
  454.7 3.3 copy-start.2
  454.7 4.2 copy-start.4
Sparse Core Ops, SparseCore 0:
  30.4 277.7 reduce-scatter.1
  311.2 133.3 all-gather.1
  448.3 512.3 all-reduce.1
where the time goes:
time: 970 us; the launch traced here: 969 us
  waiting for transfers between devices  916 us (94%)
  matrix products  17.1 us (2%)
  between operations  13.8 us (1%)
  starting transfers between devices  13.4 us (1%)
    psum x1, waiting for transfers between devices, shards(): right_gradient = lax.psum(partial_right, 'dp')  501 us
    reduce_scatter x1, waiting for transfers between devices, shards(): lax.psum_scatter(factor_part, 'dp', scatter_dimension=0, tiled=True)  271 us
    all_gather x1, waiting for transfers between devices, shards(): lax.all_gather(arrived.reshape(-1, width), 'dp', axis=0, tiled=True)  136 us
  transfers between devices with their start and end apart: 4, of which 4 were waited for; matrix products, arithmetic and copies ran while one was open for 2% of the time, Pallas kernels for 0%

commit v1 on v0

v1 whole, which is shorter than its diff:
```python
import functools

import jax
import jax.numpy as jnp
from jax import lax
from jax.experimental import pallas as pl
from jax.experimental.pallas import tpu as pltpu
from jax.sharding import PartitionSpec as P

MESH = pl.DeviceIdType.MESH
F32, BF16 = jnp.float32, jnp.bfloat16
NT = (((1,), (1,)), ((), ()))
TN = (((0,), (0,)), ((), ()))

SIZES = dict(ring=8, run=4, across=1536, chunk=1024, limit=60 * 2**20)


def kernel(
    ring, run, across, chunk,
    grad_ref, gates_ref, index_ref, state_hbm, down_hbm, left_ref, right_ref,
    hidden_hbm, left_out, right_out,
    slots, mixed, rows, down, state, hidden, right_part,
    fact_send, fact_one, fact_two_send, fact_two, fact_three_send, fact_three,
    load_sem, store_sem, own_sem, mix_send, mix_recv,
    far_recv, near_recv, far_long, far_short, near_long, near_short, run_far, run_near,
    pair_send, pair_recv, f1s, f1r, f2s, f2r, f3s, f3r,
):
    width = grad_ref.shape[1]
    tokens, top = gates_ref.shape
    experts = slots.shape[0]
    cap = slots.shape[1]
    half = ring // 2
    group = run * 2
    block = experts * cap
    batch = group * block
    rank = left_ref.shape[2]
    along = width - across
    me = lax.axis_index("expert")
    v = lax.axis_index("dp")
    y, z, c = v // group, (v // 2) % run, v % 2
    sign = 1 - 2 * c

    def at(yy, zz, cc):
        return (me, (yy * run + zz) * 2 + cc)

    def wrap(value):
        return lax.rem(value + 2 * ring, ring)

    def peer(k):
        return lax.rem(z * 2 + c + k, group)

    load_down = pltpu.make_async_copy(down_hbm.at[0], down, load_sem.at[0])
    load_state = pltpu.make_async_copy(state_hbm.at[0], state, load_sem.at[1])
    load_state.start()
    load_down.start()

    barrier = pltpu.get_barrier_semaphore()
    for k in range(1, experts):
        pl.semaphore_signal(barrier, 1, device_id=(lax.rem(me + k, experts), v), device_id_type=MESH)
    for k in range(1, ring):
        pl.semaphore_signal(barrier, 1, device_id=at(wrap(y + k), z, c), device_id_type=MESH)
    for k in range(1, group):
        pl.semaphore_signal(barrier, 1, device_id=(me, y * group + peer(k)), device_id_type=MESH)

    chosen = [[index_ref[t, k] for k in range(top)] for t in range(tokens)]
    flat = [chosen[t][k] for t in range(tokens) for k in range(top)]
    place = lax.broadcasted_iota(jnp.int32, (block, 1), 0)
    total = jnp.zeros((block, width), F32)
    for t in range(tokens):
        weight = jnp.zeros((block, 1), F32)
        for k in range(top):
            position = jnp.int32(0)
            for earlier in flat[: t * top + k]:
                position = position + (earlier == chosen[t][k]).astype(jnp.int32)
            slot = chosen[t][k] * cap + position
            weight = weight + jnp.where(place == slot, gates_ref[t, k], jnp.float32(0))
        total = total + weight * grad_ref[pl.ds(t, 1), :].astype(F32)
    total = total.astype(BF16)
    for e in range(experts):
        slots[e] = total[e * cap:(e + 1) * cap, :]

    pl.semaphore_wait(barrier, experts + ring + group - 3)

    def mix(k):
        other = lax.rem(me + k, experts)
        return pltpu.make_async_remote_copy(
            src_ref=slots.at[other], dst_ref=mixed.at[me], send_sem=mix_send.at[k],
            recv_sem=mix_recv.at[k], device_id=(other, v), device_id_type=MESH)

    for k in range(1, experts):
        mix(k).start()
    own = pltpu.make_async_copy(slots.at[me], mixed.at[me], own_sem)
    own.start()

    load_state.wait()
    part = lax.dot_general(left_ref[0], state[...], (((0,), (1,)), ((), ())), preferred_element_type=F32)
    for i in range(ring):
        fact_send[i] = part[:, i * batch:(i + 1) * batch]

    def ring_copy(src, dst, send, recv, k, slot):
        return pltpu.make_async_remote_copy(
            src_ref=src, dst_ref=dst.at[slot], send_sem=send.at[k], recv_sem=recv.at[k],
            device_id=at(wrap(y + k), z, c), device_id_type=MESH)

    def f1(k):
        return ring_copy(fact_send.at[wrap(y + k)], fact_one, f1s, f1r, k, y)

    def f2(k):
        return pltpu.make_async_remote_copy(
            src_ref=fact_two_send, dst_ref=fact_two.at[z * 2 + c], send_sem=f2s.at[k], recv_sem=f2r.at[k],
            device_id=(me, y * group + peer(k)), device_id_type=MESH)

    def f3(k):
        return ring_copy(fact_three_send, fact_three, f3s, f3r, k, y)

    for k in range(1, ring):
        f1(k).start()
    fact_one[y] = fact_send[y]

    own.wait()
    for k in range(1, experts):
        mix(k).wait_recv()
    rows[y, z, c] = jnp.concatenate([mixed[e] for e in range(experts)], axis=0)

    def piece(yy, zz, far):
        return rows.at[yy, zz, c, :, pl.ds(0, along) if far else pl.ds(along, across)]

    def step(yy, zz, far, up, send, recv):
        ref = piece(yy, zz, far)
        return pltpu.make_async_remote_copy(
            src_ref=ref, dst_ref=ref, send_sem=send, recv_sem=recv,
            device_id=at(wrap(y + up), z, c), device_id_type=MESH)

    def far_step(hop, zz, long):
        up = sign if long else -sign
        yy = wrap(y - up * hop)
        send = (far_long if long else far_short).at[hop, zz]
        return step(yy, zz, True, up, send, far_recv.at[yy, zz])

    def near_step(hop, long):
        up = sign if long else -sign
        yy = wrap(y - up * hop)
        send = (near_long if long else near_short).at[hop]
        return step(yy, z, False, up, send, near_recv.at[yy, z])

    def far_arrive(hop, zz, long):
        up = sign if long else -sign
        yy = wrap(y - up * hop)
        step(yy, zz, True, up, far_long.at[0, 0], far_recv.at[yy, zz]).wait_recv()

    def near_arrive(hop, long):
        up = sign if long else -sign
        yy = wrap(y - up * hop)
        step(yy, z, False, up, near_long.at[0], near_recv.at[yy, z]).wait_recv()

    def run_step(yy, k, far):
        ref = piece(yy, z, far)
        return pltpu.make_async_remote_copy(
            src_ref=ref, dst_ref=ref, send_sem=run_far.at[k] if far else run_near.at[yy, k],
            recv_sem=(far_recv if far else near_recv).at[yy, z],
            device_id=at(y, lax.rem(z + k, run), c), device_id_type=MESH)

    def run_arrive(yy, k, far):
        zz = lax.rem(z + run - k, run)
        ref = piece(yy, zz, far)
        pltpu.make_async_remote_copy(
            src_ref=ref, dst_ref=ref, send_sem=run_far.at[k],
            recv_sem=(far_recv if far else near_recv).at[yy, zz],
            device_id=at(y, zz, c), device_id_type=MESH).wait_recv()

    def pair(yy, cc):
        ref = rows.at[yy, :, cc]
        return pltpu.make_async_remote_copy(
            src_ref=ref, dst_ref=ref, send_sem=pair_send.at[yy], recv_sem=pair_recv.at[yy],
            device_id=at(y, z, 1 - c), device_id_type=MESH)

    near_step(0, True).start()
    near_step(0, False).start()
    far_step(0, z, True).start()
    far_step(0, z, False).start()
    for k in range(1, run):
        run_step(y, k, True).start()
    for k in range(1, run):
        run_step(y, k, False).start()

    for k in range(1, ring):
        f1(k).wait_recv()
    fact_two_send[...] = functools.reduce(lambda a, b: a + b, [fact_one[i] for i in range(ring)])
    for k in range(1, group):
        f2(k).start()
    fact_two[z * 2 + c] = fact_two_send[...]

    def near_round(hop):
        near_arrive(hop, True)
        pl.when(hop < half)(lambda: near_step(hop, True).start())
        yy = wrap(y - sign * hop)
        for k in range(1, run):
            run_step(yy, k, False).start()

        @pl.when(hop < half)
        def _():
            near_arrive(hop, False)
            pl.when(hop < half - 1)(lambda: near_step(hop, False).start())
            back = wrap(y + sign * hop)
            for k in range(1, run):
                run_step(back, k, False).start()

    for k in range(1, run):
        run_arrive(y, k, True)
        zz = lax.rem(z + run - k, run)
        far_step(0, zz, True).start()
        far_step(0, zz, False).start()
        if k == 1:
            near_round(jnp.int32(1))
    for k in range(1, group):
        f2(k).wait_recv()
    fact_three_send[...] = functools.reduce(lambda a, b: a + b, [fact_two[i] for i in range(group)])
    for k in range(1, ring):
        f3(k).start()
    fact_three[y] = fact_three_send[...]

    for k in range(1, run):
        run_arrive(y, k, False)
    pair(y, c).start()

    load_down.wait()
    left_out[0] = jnp.zeros(left_out.shape[1:], F32)

    def store(yy):
        return pltpu.make_async_copy(
            hidden.at[yy], hidden_hbm.at[0, pl.ds(pl.multiple_of(yy * batch, batch), batch), :], store_sem.at[yy])

    def compute(yy):
        pair(yy, 1 - c).wait_recv()
        factor = fact_three[yy].astype(BF16)
        units = down.shape[0]

        def body(i, carry):
            wide, low = carry
            columns = pl.ds(pl.multiple_of(i * chunk, chunk), chunk)
            x = rows[yy, :, :, :, columns].reshape(batch, chunk)
            wide = wide + lax.dot_general(x, down[:, columns], NT, preferred_element_type=F32)
            low = low + lax.dot_general(x, right_ref[0, :, columns], NT, preferred_element_type=F32)
            right_part[yy, :, columns] = jnp.dot(factor, x, preferred_element_type=F32)
            return wide, low

        wide, low = lax.fori_loop(
            0, width // chunk, body, (jnp.zeros((batch, units), F32), jnp.zeros((batch, rank), F32)))
        low = low.astype(BF16)
        delta = lax.dot_general(low, left_ref[0], NT, preferred_element_type=F32)
        hidden[yy] = (wide + 2.0 * delta).astype(BF16)
        store(yy).start()
        mine = state[pl.ds(pl.multiple_of(yy * batch, batch), batch), :]
        left_out[0] += 2.0 * lax.dot_general(mine, low, TN, preferred_element_type=F32)

    def order(n):
        hop = (n + 1) // 2
        return wrap(y + jnp.where(n % 2 == 1, -sign, sign) * hop)

    per = run // 2

    def turn(t, _):
        hop = t // 2 + 1
        odd = t % 2

        @pl.when(t < 2 * half)
        def _():
            for i in range(per):
                zz = lax.rem(z + run - (odd * per + i), run)
                far_arrive(hop, zz, True)
                pl.when(hop < half)(lambda: far_step(hop, zz, True).start())

                @pl.when(hop < half)
                def _():
                    far_arrive(hop, zz, False)
                    pl.when(hop < half - 1)(lambda: far_step(hop, zz, False).start())

            @pl.when((odd == 0) & (hop < half))
            def _():
                near_round(hop + 1)

            @pl.when(odd == 1)
            def _():
                yy = wrap(y - sign * hop)
                for k in range(1, run):
                    run_arrive(yy, k, False)
                pair(yy, c).start()

                @pl.when(hop < half)
                def _():
                    back = wrap(y + sign * hop)
                    for k in range(1, run):
                        run_arrive(back, k, False)
                    pair(back, c).start()

            @pl.when(t == 0)
            def _():
                for k in range(1, ring):
                    f3(k).wait_recv()

        @pl.when(t >= 1)
        def _():
            compute(order(t - 1))

        return 0

    lax.fori_loop(0, 2 * half + 1, turn, 0)

    right_out[0] = 2.0 * functools.reduce(lambda a, b: a + b, [right_part[i] for i in range(ring)])

    for k in range(1, experts):
        mix(k).wait_send()
    for k in range(1, ring):
        f1(k).wait_send()
        f3(k).wait_send()
    for k in range(1, group):
        f2(k).wait_send()
    for k in range(1, run):
        run_step(y, k, True).wait_send()

    def drain(i, _):
        store(i).wait()
        pair(i, c).wait_send()
        for k in range(1, run):
            run_step(i, k, False).wait_send()
        return 0

    lax.fori_loop(0, ring, drain, 0)
    for hop in range(half):
        near_step(hop, True).wait_send()
        if hop < half - 1:
            near_step(hop, False).wait_send()
        for zz in range(run):
            far_step(hop, zz, True).wait_send()
            if hop < half - 1:
                far_step(hop, zz, False).wait_send()


def shards(ring, run, across, chunk, limit, grad, gates, index, state, down, left, right):
    experts = lax.axis_size("expert")
    width = grad.shape[1]
    slots, units = state.shape[1:]
    rank = right.shape[1]
    half, group = ring // 2, run * 2
    block = slots // (ring * group)
    cap = block // experts
    batch = group * block
    dma = pltpu.SemaphoreType.DMA
    vmem = pl.BlockSpec(memory_space=pltpu.VMEM)
    smem = pl.BlockSpec(memory_space=pltpu.SMEM)
    hbm = pl.BlockSpec(memory_space=pl.ANY)
    return pl.pallas_call(
        functools.partial(kernel, ring, run, across, chunk),
        out_shape=(
            jax.ShapeDtypeStruct((1, slots, units), BF16),
            jax.ShapeDtypeStruct((1, units, rank), F32),
            jax.ShapeDtypeStruct((1, rank, width), F32),
        ),
        in_specs=[vmem, smem, smem, hbm, hbm, vmem, vmem],
        out_specs=(hbm, vmem, vmem),
        scratch_shapes=[
            pltpu.VMEM((experts, cap, width), BF16),
            pltpu.VMEM((experts, cap, width), BF16),
            pltpu.VMEM((ring, run, 2, block, width), BF16),
            pltpu.VMEM((units, width), BF16),
            pltpu.VMEM((slots, units), BF16),
            pltpu.VMEM((ring, batch, units), BF16),
            pltpu.VMEM((ring, rank, width), F32),
            pltpu.VMEM((ring, rank, batch), F32),
            pltpu.VMEM((ring, rank, batch), F32),
            pltpu.VMEM((rank, batch), F32),
            pltpu.VMEM((group, rank, batch), F32),
            pltpu.VMEM((rank, batch), F32),
            pltpu.VMEM((ring, rank, batch), F32),
            dma((2,)), dma((ring,)), dma, dma((experts,)), dma((experts,)),
            dma((ring, run)), dma((ring, run)), dma((half, run)), dma((half, run)),
            dma((half,)), dma((half,)), dma((run,)), dma((ring, run)),
            dma((ring,)), dma((ring,)),
            dma((ring,)), dma((ring,)), dma((group,)), dma((group,)), dma((ring,)), dma((ring,)),
        ],
        compiler_params=pltpu.CompilerParams(
            collective_id=0, has_side_effects=True, vmem_limit_bytes=limit),
    )(grad, gates, index, state, down, left, right)


def solution(mesh, **sizes):
    in_specs = (
        P(("expert", "dp"), None),
        P(("expert", "dp"), None),
        P(("expert", "dp"), None),
        P("expert", None, "dp"),
        P("expert", "dp", None),
        P("expert", "dp", None),
        P("expert", None, None),
    )
    out_specs = (P("expert", None, "dp"), P("expert", "dp", None), P("expert", None, None))
    sizes = dict(SIZES, **sizes)
    body = functools.partial(
        shards, sizes["ring"], sizes["run"], sizes["across"], sizes["chunk"], sizes["limit"])
    return jax.shard_map(body, mesh=mesh, in_specs=in_specs, out_specs=out_specs, check_vma=False)
```

time: 970 us -> 104 us (0.11)
  waiting for transfers between devices: 916 us -> 0 us
  Pallas kernels: 0 us -> 93.9 us
  matrix products: 17.1 us -> 0 us
  starting transfers between devices: 13.4 us -> 0 us
  between operations: 13.8 us -> 0.64 us
    psum x1 -> x0, waiting for transfers between devices: 501 us -> none  [shards(): right_gradient = lax.psum(partial_right, 'dp')]
    reduce_scatter x1 -> x0, waiting for transfers between devices: 271 us -> none  [shards(): lax.psum_scatter(factor_part, 'dp', scatter_dimension=0, tiled=True)]
    all_gather x1 -> x0, waiting for transfers between devices: 136 us -> none  [shards(): lax.all_gather(arrived.reshape(-1, width), 'dp', axis=0, tiled=True)]
    pallas_call x0 -> x1, Pallas kernels: none -> 93.9 us  [shards(): pl.pallas_call(functools.partial(kernel, ring, run, across, chunk), out_s...]
    dot_general x6 -> x0, matrix products: 17.1 us -> none  [the longest x1 7.79 us: shards(): lax.dot_general(gathered, weight_slice, (((1,), (1,)), ((), ())), preferr...]
    all_to_all x1 -> x0, starting transfers between devices: 13.3 us -> none  [shards(): lax.all_to_all(send_buffer, 'expert', split_axis=0, concat_axis=0, tiled=...]
  transfers between devices with their start and end apart: 4 -> 0, of which waited for: 4 -> 0; matrix products, arithmetic and copies ran while one was open for 2% -> 0% of each run, Pallas kernels for 0% -> 0%
where the time goes in v1:
time: 104 us
  Pallas kernels  93.9 us (90%)
  local copies, waits for them, and re-layouts  9.32 us (9%)
    pallas_call x1, Pallas kernels, shards(): pl.pallas_call(functools.partial(kernel, ring, run, across, chunk), out_s...  93.9 us
    unnamed x5, local copies, waits for them, and re-layouts  7.73 us

profile of v1, /device:TPU:1, one launch (start us, length us, event | category | flops | bytes accessed | tf_op | source)
XLA Modules:
  0.0 103.9 jit_solution(8122472668779835367)
XLA Ops:
  0.6 1.3 %copy.10.gates_ref = f32[4,2]{1,0:T(4,128)} copy(f32[4,2]{0,1:T(2,128)} %param.8) | data formatting | bytes 64 | tf_op args[1]
  2.0 1.3 %copy.11.index_ref = s32[4,2]{1,0:T(4,128)} copy(s32[4,2]{0,1:T(2,128)} %param.9) | data formatting | bytes 64 | tf_op args[2]
  3.3 1.4 %copy.12.left_ref = bf16[1,256,16]{2,1,0:T(8,128)(2,1)} copy(bf16[1,256,16]{1,2,0:T(8,128)(2,1)} %param.12) | data formatting | bytes 16384 | tf_op args[5]
  4.7 93.9 %shard_map.94 = (bf16[1,1024,256]{2,1,0:T(8,128)(2,1)}, f32[1,256,16]{2,1,0:T(8,128)}, f32[1,16,6144]{2,1,0:T(8,128)}) custom-call(bf16[4,6144]{1,0:T(4,128)(2,1)} %grad_ref.1, f32[4,2]{1,0:T(4,128)} %copy.10.gates_ref, s32[4,2]{1,0:T(4,128)} %copy.11.index_ref, bf16[1,1024,256]{2,1,0:T(8,128)(2,1)} %state_hbm.1, bf16[1,256,6144]{2,1,0:T(8,128)(2,1)} %down_hbm.1, ...), custom_call_target="tpu_custom_call" | custom-call | tf_op jit(solution)/shard_map/pallas_call | solution.py:352
  98.6 1.6 %copy.13 = f32[1,256,16]{1,2,0:T(8,128)} copy(f32[1,256,16]{2,1,0:T(8,128)} %get-tuple-element.4) | data formatting | bytes 32768 | tf_op jit(solution)/shard_map/pallas_call | solution.py:352
  100.2 1.9 %copy.16 = bf16[1,1024,256]{2,1,0:T(8,128)(2,1)} copy(bf16[1,1024,256]{2,1,0:T(8,128)(2,1)} %get-tuple-element.9) | data formatting | bytes 1048576
  102.1 1.8 %copy.17 = f32[1,16,6144]{2,1,0:T(8,128)} copy(f32[1,16,6144]{2,1,0:T(8,128)} %get-tuple-element.11) | data formatting | bytes 786432

commit v2 on v1

--- a/solution.py
+++ b/solution.py
@@ -26,14 +26,14 @@
     pair_send, pair_recv, f1s, f1r, f2s, f2r, f3s, f3r,
 ):
     width = grad_ref.shape[1]
-    tokens, top = gates_ref.shape
+    top, tokens = gates_ref.shape
     experts = slots.shape[0]
     cap = slots.shape[1]
     half = ring // 2
     group = run * 2
     block = experts * cap
     batch = group * block
-    rank = left_ref.shape[2]
+    rank = left_ref.shape[1]
     along = width - across
     me = lax.axis_index("expert")
     v = lax.axis_index("dp")
@@ -62,7 +62,7 @@
     for k in range(1, group):
         pl.semaphore_signal(barrier, 1, device_id=(me, y * group + peer(k)), device_id_type=MESH)
 
-    chosen = [[index_ref[t, k] for k in range(top)] for t in range(tokens)]
+    chosen = [[index_ref[k, t] for k in range(top)] for t in range(tokens)]
     flat = [chosen[t][k] for t in range(tokens) for k in range(top)]
     place = lax.broadcasted_iota(jnp.int32, (block, 1), 0)
     total = jnp.zeros((block, width), F32)
@@ -73,7 +73,7 @@
             for earlier in flat[: t * top + k]:
                 position = position + (earlier == chosen[t][k]).astype(jnp.int32)
             slot = chosen[t][k] * cap + position
-            weight = weight + jnp.where(place == slot, gates_ref[t, k], jnp.float32(0))
+            weight = weight + jnp.where(place == slot, gates_ref[k, t], jnp.float32(0))
         total = total + weight * grad_ref[pl.ds(t, 1), :].astype(F32)
     total = total.astype(BF16)
     for e in range(experts):
@@ -93,7 +93,7 @@
     own.start()
 
     load_state.wait()
-    part = lax.dot_general(left_ref[0], state[...], (((0,), (1,)), ((), ())), preferred_element_type=F32)
+    part = lax.dot_general(left_ref[0], state[...], NT, preferred_element_type=F32)
     for i in range(ring):
         fact_send[i] = part[:, i * batch:(i + 1) * batch]
 
@@ -190,34 +190,49 @@
         f2(k).start()
     fact_two[z * 2 + c] = fact_two_send[...]
 
-    def near_round(hop):
+    def near_turn(hop):
         near_arrive(hop, True)
-        pl.when(hop < half)(lambda: near_step(hop, True).start())
-        yy = wrap(y - sign * hop)
+        if hop < half:
+            near_step(hop, True).start()
+            near_arrive(hop, False)
+            if hop < half - 1:
+                near_step(hop, False).start()
+
+    def near_out(hop):
         for k in range(1, run):
-            run_step(yy, k, False).start()
+            run_step(wrap(y - sign * hop), k, False).start()
+        if hop < half:
+            for k in range(1, run):
+                run_step(wrap(y + sign * hop), k, False).start()
+
+    def far_turn(hop, zz):
+        far_arrive(hop, zz, True)
+        pl.when(hop < half)(lambda: far_step(hop, zz, True).start())
 
         @pl.when(hop < half)
         def _():
-            near_arrive(hop, False)
-            pl.when(hop < half - 1)(lambda: near_step(hop, False).start())
-            back = wrap(y + sign * hop)
+            far_arrive(hop, zz, False)
+            pl.when(hop < half - 1)(lambda: far_step(hop, zz, False).start())
+
+    for hop in range(1, half + 1):
+        near_turn(hop)
+        far_turn(jnp.int32(hop), z)
+        if hop == half // 2:
             for k in range(1, run):
-                run_step(back, k, False).start()
-
-    for k in range(1, run):
-        run_arrive(y, k, True)
-        zz = lax.rem(z + run - k, run)
-        far_step(0, zz, True).start()
-        far_step(0, zz, False).start()
-        if k == 1:
-            near_round(jnp.int32(1))
-    for k in range(1, group):
-        f2(k).wait_recv()
-    fact_three_send[...] = functools.reduce(lambda a, b: a + b, [fact_two[i] for i in range(group)])
-    for k in range(1, ring):
-        f3(k).start()
-    fact_three[y] = fact_three_send[...]
+                run_arrive(y, k, True)
+                zz = lax.rem(z + run - k, run)
+                far_step(0, zz, True).start()
+                far_step(0, zz, False).start()
+            for k in range(1, group):
+                f2(k).wait_recv()
+            fact_three_send[...] = functools.reduce(lambda a, b: a + b, [fact_two[i] for i in range(group)])
+            for k in range(1, ring):
+                f3(k).start()
+            fact_three[y] = fact_three_send[...]
+            for earlier in range(1, hop):
+                near_out(earlier)
+        if hop >= half // 2:
+            near_out(hop)
 
     for k in range(1, run):
         run_arrive(y, k, False)
@@ -247,64 +262,57 @@
         wide, low = lax.fori_loop(
             0, width // chunk, body, (jnp.zeros((batch, units), F32), jnp.zeros((batch, rank), F32)))
         low = low.astype(BF16)
-        delta = lax.dot_general(low, left_ref[0], NT, preferred_element_type=F32)
+        delta = jnp.dot(low, left_ref[0], preferred_element_type=F32)
         hidden[yy] = (wide + 2.0 * delta).astype(BF16)
         store(yy).start()
         mine = state[pl.ds(pl.multiple_of(yy * batch, batch), batch), :]
-        left_out[0] += 2.0 * lax.dot_general(mine, low, TN, preferred_element_type=F32)
+        left_out[0] += 2.0 * lax.dot_general(low, mine, TN, preferred_element_type=F32)
 
     def order(n):
         hop = (n + 1) // 2
         return wrap(y + jnp.where(n % 2 == 1, -sign, sign) * hop)
 
-    per = run // 2
+    first = run // 2
 
     def turn(t, _):
         hop = t // 2 + 1
-        odd = t % 2
-
-        @pl.when(t < 2 * half)
+
+        @pl.when(t % 2 == 0)
         def _():
-            for i in range(per):
-                zz = lax.rem(z + run - (odd * per + i), run)
-                far_arrive(hop, zz, True)
-                pl.when(hop < half)(lambda: far_step(hop, zz, True).start())
-
-                @pl.when(hop < half)
-                def _():
-                    far_arrive(hop, zz, False)
-                    pl.when(hop < half - 1)(lambda: far_step(hop, zz, False).start())
-
-            @pl.when((odd == 0) & (hop < half))
+            for k in range(1, first):
+                far_turn(hop, lax.rem(z + run - k, run))
+
+        @pl.when(t % 2 == 1)
+        def _():
+            for k in range(first, run):
+                far_turn(hop, lax.rem(z + run - k, run))
+            yy = wrap(y - sign * hop)
+            for k in range(1, run):
+                run_arrive(yy, k, False)
+            pair(yy, c).start()
+
+            @pl.when(hop < half)
             def _():
-                near_round(hop + 1)
-
-            @pl.when(odd == 1)
-            def _():
-                yy = wrap(y - sign * hop)
+                back = wrap(y + sign * hop)
                 for k in range(1, run):
-                    run_arrive(yy, k, False)
-                pair(yy, c).start()
-
-                @pl.when(hop < half)
-                def _():
-                    back = wrap(y + sign * hop)
-                    for k in range(1, run):
-                        run_arrive(back, k, False)
-                    pair(back, c).start()
-
-            @pl.when(t == 0)
-            def _():
-                for k in range(1, ring):
-                    f3(k).wait_recv()
-
-        @pl.when(t >= 1)
+                    run_arrive(back, k, False)
+                pair(back, c).start()
+
+        @pl.when(t == 0)
         def _():
-            compute(order(t - 1))
-
+            for k in range(1, ring):
+                f3(k).wait_recv()
+
+        def one(n, _):
+            compute(order(n))
+            return 0
+
+        start = jnp.where(t < 2 * half - 1, jnp.maximum(t - 1, 0), ring - 1)
+        lax.fori_loop(start, jnp.where(t < 2 * half - 2, t, ring - 1), one, 0)
         return 0
 
-    lax.fori_loop(0, 2 * half + 1, turn, 0)
+    lax.fori_loop(0, 2 * half, turn, 0)
+    compute(order(ring - 1))
 
     right_out[0] = 2.0 * functools.reduce(lambda a, b: a + b, [right_part[i] for i in range(ring)])
 
@@ -334,6 +342,19 @@
             far_step(hop, zz, True).wait_send()
             if hop < half - 1:
                 far_step(hop, zz, False).wait_send()
+
+
+def finish(a, b, c, a_out, b_out, c_out, a_mid, b_mid, c_mid, load, store):
+    parts = [(a, a_mid, a_out), (b, b_mid, b_out), (c, c_mid, c_out)]
+    loads = [pltpu.make_async_copy(x, m, load.at[i]) for i, (x, m, o) in enumerate(parts)]
+    stores = [pltpu.make_async_copy(m, o, store.at[i]) for i, (x, m, o) in enumerate(parts)]
+    for copy in loads:
+        copy.start()
+    for copy, after in zip(loads, stores):
+        copy.wait()
+        after.start()
+    for copy in stores:
+        copy.wait()
 
 
 def shards(ring, run, across, chunk, limit, grad, gates, index, state, down, left, right):
@@ -349,11 +370,11 @@
     vmem = pl.BlockSpec(memory_space=pltpu.VMEM)
     smem = pl.BlockSpec(memory_space=pltpu.SMEM)
     hbm = pl.BlockSpec(memory_space=pl.ANY)
-    return pl.pallas_call(
+    results = pl.pallas_call(
         functools.partial(kernel, ring, run, across, chunk),
         out_shape=(
             jax.ShapeDtypeStruct((1, slots, units), BF16),
-            jax.ShapeDtypeStruct((1, units, rank), F32),
+            jax.ShapeDtypeStruct((1, rank, units), F32),
             jax.ShapeDtypeStruct((1, rank, width), F32),
         ),
         in_specs=[vmem, smem, smem, hbm, hbm, vmem, vmem],
@@ -380,7 +401,16 @@
         ],
         compiler_params=pltpu.CompilerParams(
             collective_id=0, has_side_effects=True, vmem_limit_bytes=limit),
-    )(grad, gates, index, state, down, left, right)
+    )(grad, gates.T, index.T, state, down, jnp.swapaxes(left, 1, 2), right)
+    hidden_gradient, left_gradient, right_gradient = pl.pallas_call(
+        finish,
+        out_shape=tuple(jax.ShapeDtypeStruct(r.shape, r.dtype) for r in results),
+        in_specs=[hbm] * 3,
+        out_specs=(hbm,) * 3,
+        scratch_shapes=[pltpu.VMEM(r.shape, r.dtype) for r in results] + [dma((3,)), dma((3,))],
+        compiler_params=pltpu.CompilerParams(vmem_limit_bytes=limit),
+    )(*results)
+    return hidden_gradient, jnp.swapaxes(left_gradient, 1, 2), right_gradient
 
 
 def solution(mesh, **sizes):

time: 104 us -> 92.5 us (0.89)
  local copies, waits for them, and re-layouts: 9.32 us -> 0 us
  Pallas kernels: 93.9 us -> 91.5 us
    unnamed x5 -> x0, local copies, waits for them, and re-layouts: 7.73 us -> none
    pallas_call x1, Pallas kernels: 93.9 us -> 89.5 us  [shards(): pl.pallas_call(functools.partial(kernel, ring, run, across, chunk), out_s...]
    pallas_call x0 -> x1, Pallas kernels: none -> 2.02 us  [shards(): pl.pallas_call(finish, out_shape=tuple((jax.ShapeDtypeStruct(r.shape, r.d...]
    pallas_call x1 -> x0, local copies, waits for them, and re-layouts: 1.58 us -> none  [shards(): pl.pallas_call(functools.partial(kernel, ring, run, across, chunk), out_s...]
where the time goes in v2:
time: 92.5 us; the launch traced here: 92.1 us
  Pallas kernels  91.5 us (99%)
    pallas_call x1, Pallas kernels, shards(): pl.pallas_call(functools.partial(kernel, ring, run, across, chunk), out_s...  89.5 us
    pallas_call x1, Pallas kernels, shards(): pl.pallas_call(finish, out_shape=tuple((jax.ShapeDtypeStruct(r.shape, r.d...  2.02 us

profile of v2, /device:TPU:1, one launch (start us, length us, event | category | flops | bytes accessed | tf_op | source)
XLA Modules:
  0.0 92.1 jit_solution(17790927790741924584)
XLA Ops:
  0.6 89.5 %shard_map.94 = (bf16[1,1024,256]{2,1,0:T(8,128)(2,1)}, f32[1,16,256]{2,1,0:T(8,128)}, f32[1,16,6144]{2,1,0:T(8,128)}) custom-call(bf16[4,6144]{1,0:T(4,128)(2,1)} %grad_ref.1, f32[2,4]{1,0:T(2,128)} %bitcast.5, s32[2,4]{1,0:T(2,128)} %bitcast.6, bf16[1,1024,256]{2,1,0:T(8,128)(2,1)} %state_hbm.1, bf16[1,256,6144]{2,1,0:T(8,128)(2,1)} %down_hbm.1, ...), custom_call_target="tpu_custom_call" | custom-call | tf_op jit(solution)/shard_map/pallas_call | solution.py:373
  90.1 2.0 %shard_map.95 = (bf16[1,1024,256]{2,1,0:T(8,128)(2,1)}, f32[1,16,256]{2,1,0:T(8,128)}, f32[1,16,6144]{2,1,0:T(8,128)}) custom-call(bf16[1,1024,256]{2,1,0:T(8,128)(2,1)} %get-tuple-element.9.a, f32[1,16,256]{2,1,0:T(8,128)} %get-tuple-element.10.b, f32[1,16,6144]{2,1,0:T(8,128)} %get-tuple-element.11.c), custom_call_target="tpu_custom_call" | custom-call | tf_op jit(solution)/shard_map/pallas_call | solution.py:405

commit v3 on v2

--- a/solution.py
+++ b/solution.py
@@ -12,7 +12,7 @@
 NT = (((1,), (1,)), ((), ()))
 TN = (((0,), (0,)), ((), ()))
 
-SIZES = dict(ring=8, run=4, across=1536, chunk=1024, limit=60 * 2**20)
+SIZES = dict(ring=8, run=4, across=1536, chunk=3072, limit=60 * 2**20)
 
 
 def kernel(

time: 92.5 us -> 89.6 us (0.969)
  Pallas kernels: 91.5 us -> 88.8 us
    pallas_call x1, Pallas kernels: 89.5 us -> 86.7 us  [shards(): pl.pallas_call(functools.partial(kernel, ring, run, across, chunk), out_s...]
where the time goes in v3:
time: 89.6 us; the launch traced here: 89.4 us
  Pallas kernels  88.8 us (99%)
    pallas_call x1, Pallas kernels, shards(): pl.pallas_call(functools.partial(kernel, ring, run, across, chunk), out_s...  86.7 us
    pallas_call x1, Pallas kernels, shards(): pl.pallas_call(finish, out_shape=tuple((jax.ShapeDtypeStruct(r.shape, r.d...  2.02 us

profile of v3, /device:TPU:1, one launch (start us, length us, event | category | flops | bytes accessed | tf_op | source)
XLA Modules:
  0.0 89.4 jit_solution(8635950250610469213)
XLA Ops:
  0.6 86.7 %shard_map.94 = (bf16[1,1024,256]{2,1,0:T(8,128)(2,1)}, f32[1,16,256]{2,1,0:T(8,128)}, f32[1,16,6144]{2,1,0:T(8,128)}) custom-call(bf16[4,6144]{1,0:T(4,128)(2,1)} %grad_ref.1, f32[2,4]{1,0:T(2,128)} %bitcast.5, s32[2,4]{1,0:T(2,128)} %bitcast.6, bf16[1,1024,256]{2,1,0:T(8,128)(2,1)} %state_hbm.1, bf16[1,256,6144]{2,1,0:T(8,128)(2,1)} %down_hbm.1, ...), custom_call_target="tpu_custom_call" | custom-call | tf_op jit(solution)/shard_map/pallas_call | solution.py:373
  87.4 2.0 %shard_map.95 = (bf16[1,1024,256]{2,1,0:T(8,128)(2,1)}, f32[1,16,256]{2,1,0:T(8,128)}, f32[1,16,6144]{2,1,0:T(8,128)}) custom-call(bf16[1,1024,256]{2,1,0:T(8,128)(2,1)} %get-tuple-element.9.a, f32[1,16,256]{2,1,0:T(8,128)} %get-tuple-element.10.b, f32[1,16,6144]{2,1,0:T(8,128)} %get-tuple-element.11.c), custom_call_target="tpu_custom_call" | custom-call | tf_op jit(solution)/shard_map/pallas_call | solution.py:405

commit v4 on v3

--- a/solution.py
+++ b/solution.py
@@ -312,10 +312,6 @@
         return 0
 
     lax.fori_loop(0, 2 * half, turn, 0)
-    compute(order(ring - 1))
-
-    right_out[0] = 2.0 * functools.reduce(lambda a, b: a + b, [right_part[i] for i in range(ring)])
-
     for k in range(1, experts):
         mix(k).wait_send()
     for k in range(1, ring):
@@ -327,8 +323,6 @@
         run_step(y, k, True).wait_send()
 
     def drain(i, _):
-        store(i).wait()
-        pair(i, c).wait_send()
         for k in range(1, run):
             run_step(i, k, False).wait_send()
         return 0
@@ -342,6 +336,17 @@
             far_step(hop, zz, True).wait_send()
             if hop < half - 1:
                 far_step(hop, zz, False).wait_send()
+
+    compute(order(ring - 1))
+
+    right_out[0] = 2.0 * functools.reduce(lambda a, b: a + b, [right_part[i] for i in range(ring)])
+
+    def finished(i, _):
+        store(i).wait()
+        pair(i, c).wait_send()
+        return 0
+
+    lax.fori_loop(0, ring, finished, 0)
 
 
 def finish(a, b, c, a_out, b_out, c_out, a_mid, b_mid, c_mid, load, store):

time: 89.6 us -> 89.5 us (level)
  no operation moved by 1% of the time
where the time goes in v4:
time: 89.5 us; the launch traced here: 89.3 us
  Pallas kernels  88.7 us (99%)
    pallas_call x1, Pallas kernels, shards(): pl.pallas_call(functools.partial(kernel, ring, run, across, chunk), out_s...  86.7 us
    pallas_call x1, Pallas kernels, shards(): pl.pallas_call(finish, out_shape=tuple((jax.ShapeDtypeStruct(r.shape, r.d...  2.02 us

profile of v4, /device:TPU:1, one launch (start us, length us, event | category | flops | bytes accessed | tf_op | source)
XLA Modules:
  0.0 89.3 jit_solution(9472069020782049825)
XLA Ops:
  0.6 86.7 %shard_map.94 = (bf16[1,1024,256]{2,1,0:T(8,128)(2,1)}, f32[1,16,256]{2,1,0:T(8,128)}, f32[1,16,6144]{2,1,0:T(8,128)}) custom-call(bf16[4,6144]{1,0:T(4,128)(2,1)} %grad_ref.1, f32[2,4]{1,0:T(2,128)} %bitcast.5, s32[2,4]{1,0:T(2,128)} %bitcast.6, bf16[1,1024,256]{2,1,0:T(8,128)(2,1)} %state_hbm.1, bf16[1,256,6144]{2,1,0:T(8,128)(2,1)} %down_hbm.1, ...), custom_call_target="tpu_custom_call" | custom-call | tf_op jit(solution)/shard_map/pallas_call | solution.py:378
  87.3 2.0 %shard_map.95 = (bf16[1,1024,256]{2,1,0:T(8,128)(2,1)}, f32[1,16,256]{2,1,0:T(8,128)}, f32[1,16,6144]{2,1,0:T(8,128)}) custom-call(bf16[1,1024,256]{2,1,0:T(8,128)(2,1)} %get-tuple-element.9.a, f32[1,16,256]{2,1,0:T(8,128)} %get-tuple-element.10.b, f32[1,16,6144]{2,1,0:T(8,128)} %get-tuple-element.11.c), custom_call_target="tpu_custom_call" | custom-call | tf_op jit(solution)/shard_map/pallas_call | solution.py:410

commit v5 on v3

--- a/solution.py
+++ b/solution.py
@@ -17,9 +17,9 @@
 
 def kernel(
     ring, run, across, chunk,
-    grad_ref, gates_ref, index_ref, state_hbm, down_hbm, left_ref, right_ref,
+    grad_hbm, gates_ref, index_ref, state_hbm, down_hbm, left_hbm, right_hbm,
     hidden_hbm, left_out, right_out,
-    slots, mixed, rows, down, state, hidden, right_part,
+    grad_ref, left_ref, right_ref, slots, mixed, rows, down, state, hidden, right_part,
     fact_send, fact_one, fact_two_send, fact_two, fact_three_send, fact_three,
     load_sem, store_sem, own_sem, mix_send, mix_recv,
     far_recv, near_recv, far_long, far_short, near_long, near_short, run_far, run_near,
@@ -51,8 +51,6 @@
 
     load_down = pltpu.make_async_copy(down_hbm.at[0], down, load_sem.at[0])
     load_state = pltpu.make_async_copy(state_hbm.at[0], state, load_sem.at[1])
-    load_state.start()
-    load_down.start()
 
     barrier = pltpu.get_barrier_semaphore()
     for k in range(1, experts):
@@ -61,6 +59,16 @@
         pl.semaphore_signal(barrier, 1, device_id=at(wrap(y + k), z, c), device_id_type=MESH)
     for k in range(1, group):
         pl.semaphore_signal(barrier, 1, device_id=(me, y * group + peer(k)), device_id_type=MESH)
+
+    loads = [
+        pltpu.make_async_copy(src, dst, load_sem.at[2 + i])
+        for i, (src, dst) in enumerate([(grad_hbm, grad_ref), (left_hbm, left_ref), (right_hbm, right_ref)])
+    ]
+    for load in loads:
+        load.start()
+    load_state.start()
+    load_down.start()
+    loads[0].wait()
 
     chosen = [[index_ref[k, t] for k in range(top)] for t in range(tokens)]
     flat = [chosen[t][k] for t in range(tokens) for k in range(top)]
@@ -93,6 +101,8 @@
     own.start()
 
     load_state.wait()
+    loads[1].wait()
+    loads[2].wait()
     part = lax.dot_general(left_ref[0], state[...], NT, preferred_element_type=F32)
     for i in range(ring):
         fact_send[i] = part[:, i * batch:(i + 1) * batch]
@@ -377,9 +387,12 @@
             jax.ShapeDtypeStruct((1, rank, units), F32),
             jax.ShapeDtypeStruct((1, rank, width), F32),
         ),
-        in_specs=[vmem, smem, smem, hbm, hbm, vmem, vmem],
+        in_specs=[hbm, smem, smem, hbm, hbm, hbm, hbm],
         out_specs=(hbm, vmem, vmem),
         scratch_shapes=[
+            pltpu.VMEM(grad.shape, BF16),
+            pltpu.VMEM((1, rank, units), BF16),
+            pltpu.VMEM(right.shape, BF16),
             pltpu.VMEM((experts, cap, width), BF16),
             pltpu.VMEM((experts, cap, width), BF16),
             pltpu.VMEM((ring, run, 2, block, width), BF16),
@@ -393,7 +406,7 @@
             pltpu.VMEM((group, rank, batch), F32),
             pltpu.VMEM((rank, batch), F32),
             pltpu.VMEM((ring, rank, batch), F32),
-            dma((2,)), dma((ring,)), dma, dma((experts,)), dma((experts,)),
+            dma((5,)), dma((ring,)), dma, dma((experts,)), dma((experts,)),
             dma((ring, run)), dma((ring, run)), dma((half, run)), dma((half, run)),
             dma((half,)), dma((half,)), dma((run,)), dma((ring, run)),
             dma((ring,)), dma((ring,)),

time: 89.6 us -> 89.3 us (level)
  no operation moved by 1% of the time
where the time goes in v5:
time: 89.3 us; the launch traced here: 89.2 us
  Pallas kernels  88.5 us (99%)
    pallas_call x1, Pallas kernels, shards(): pl.pallas_call(functools.partial(kernel, ring, run, across, chunk), out_s...  86.5 us
    pallas_call x1, Pallas kernels, shards(): pl.pallas_call(finish, out_shape=tuple((jax.ShapeDtypeStruct(r.shape, r.d...  2.02 us

profile of v5, /device:TPU:1, one launch (start us, length us, event | category | flops | bytes accessed | tf_op | source)
XLA Modules:
  0.0 89.2 jit_solution(5929113019118138799)
XLA Ops:
  0.6 86.5 %shard_map.94 = (bf16[1,1024,256]{2,1,0:T(8,128)(2,1)}, f32[1,16,256]{2,1,0:T(8,128)}, f32[1,16,6144]{2,1,0:T(8,128)}) custom-call(bf16[4,6144]{1,0:T(4,128)(2,1)} %grad_hbm.1, f32[2,4]{1,0:T(2,128)} %bitcast.5, s32[2,4]{1,0:T(2,128)} %bitcast.6, bf16[1,1024,256]{2,1,0:T(8,128)(2,1)} %state_hbm.1, bf16[1,256,6144]{2,1,0:T(8,128)(2,1)} %down_hbm.1, ...), custom_call_target="tpu_custom_call" | custom-call | tf_op jit(solution)/shard_map/pallas_call | solution.py:383
  87.1 2.0 %shard_map.95 = (bf16[1,1024,256]{2,1,0:T(8,128)(2,1)}, f32[1,16,256]{2,1,0:T(8,128)}, f32[1,16,6144]{2,1,0:T(8,128)}) custom-call(bf16[1,1024,256]{2,1,0:T(8,128)(2,1)} %get-tuple-element.9.a, f32[1,16,256]{2,1,0:T(8,128)} %get-tuple-element.10.b, f32[1,16,6144]{2,1,0:T(8,128)} %get-tuple-element.11.c), custom_call_target="tpu_custom_call" | custom-call | tf_op jit(solution)/shard_map/pallas_call | solution.py:418
